TPU v7x, 512 devices: a whole 4x4x16 slice. The times are simulated.
512 devices in a mesh: grp: 64 (over x, z), dev: 8 (over y, core).
Axes of the slice: x: 4, y: 4, z: 16, core: 2. Of those that a mesh axis runs over, the one named last changes fastest.
Arguments:
- tokens: bfloat16 [32768, 768], P(('grp', 'dev')), may hold values from -6 to 6
- expert_ids: int32 [32768, 8], P(('grp', 'dev')), may hold values from 0 to 511, as said below
- gates: bfloat16 [32768, 8], P(('grp', 'dev')), may hold values from 0.099609375 to 0.5
- w_in: bfloat16 [512, 768, 1536], P(('grp', 'dev')), may hold values from -0.21875 to 0.21875
- w_out: bfloat16 [512, 1536, 768], P(('grp', 'dev')), may hold values from -0.15625 to 0.15625
Outputs:
- mixed: bfloat16 [32768, 768], P(('grp', 'dev'))
Inputs may be any that keep to these rules, and one draw needn't show every extreme that they name: `expert_ids`: row t lists 8 experts; columns 2 * k and 2 * k + 1 are two different experts of one group (experts g * 8 to g * 8 + 7 form group g), and the four groups of a row differ. The owner of token t is t // 64, and its dev index is the owner modulo 8. The tokens of one owner pick one group at most 12 times, and every owner reaches it for some group. The tokens whose owners share a dev index pick each group exactly 4 * 64 times in all and each expert at most 192 times; in every group one expert is picked 192 times by the tokens of every dev index.
All inputs are finite; a program needn't handle non-finite values.
Results may differ from a plain program's by a relative error of at most 0.0057.
Values may be sent and summed in bfloat16 or wider, within the bound.
A program may use at most 64 MiB of HBM per device.

v0:
```python
import jax
import jax.numpy as jnp
from jax import lax
from jax.sharding import PartitionSpec as P


def earlier_count(onehot):
    return jnp.cumsum(onehot, axis=0) - onehot


def contract_rows(left, right):
    return lax.dot_general(
        left,
        right,
        (((0,), (0,)), ((), ())),
        precision=lax.Precision.HIGHEST,
        preferred_element_type=jnp.float32,
    )


def expert_rows(slot_block, w_first, w_second):

    def one_block(rows_block):
        hidden = jnp.maximum(
            jnp.dot(rows_block, w_first, preferred_element_type=jnp.float32), 0.0
        ).astype(jnp.bfloat16)
        return jnp.dot(hidden, w_second, preferred_element_type=jnp.float32).astype(jnp.bfloat16)

    return lax.map(one_block, slot_block)


def seat_sources(seat_of, valid, seat_total):
    item_count = seat_of.shape[0]
    target_seat = jnp.where(valid, seat_of, seat_total)
    empty_seats = jnp.full((seat_total,), item_count, jnp.int32)
    return empty_seats.at[target_seat].set(jnp.arange(item_count, dtype=jnp.int32), mode="drop")


def per_device(tokens, expert_ids, gates, w_in, w_out):
    n_grp = lax.axis_size("grp")
    n_dev = lax.axis_size("dev")
    token_count, feature_width = tokens.shape
    cap_grp = min(token_count, 3 * ((4 * token_count + n_grp - 1) // n_grp))
    cap_exp = min(4 * token_count, 24 * token_count // n_dev)
    seat_total = n_dev * cap_exp
    zero_half = jnp.zeros((), jnp.bfloat16)
    w_first = w_in[0]
    w_second = w_out[0]
    pair_ids = expert_ids.reshape(token_count * 4, 2)
    pair_group = pair_ids[:, 0] // n_dev
    group_hot = (pair_group[:, None] == jnp.arange(n_grp)[None, :]).astype(jnp.int32)
    group_rank = jnp.sum(earlier_count(group_hot) * group_hot, axis=1)
    target = pair_group * cap_grp + group_rank
    slot_count = n_grp * cap_grp
    placed = (target[None, :] == jnp.arange(slot_count)[:, None]).astype(jnp.int32)
    token_hot = placed.reshape(slot_count, token_count, 4).sum(axis=2)
    rows_out = jnp.dot(
        token_hot.astype(jnp.bfloat16), tokens, preferred_element_type=jnp.float32
    ).astype(jnp.bfloat16)
    local_ids = pair_ids % n_dev
    picks_out = jnp.dot(placed, local_ids + 1) - 1
    gains_out = jnp.dot(
        placed.astype(jnp.bfloat16),
        gates.reshape(token_count * 4, 2),
        preferred_element_type=jnp.float32,
    ).astype(jnp.bfloat16)
    rows_in, picks_in, gains_in = (
        lax.all_to_all(
            rows_out.reshape(n_grp, cap_grp, feature_width),
            "grp",
            split_axis=0,
            concat_axis=0,
            tiled=True,
        ),
        lax.all_to_all(
            picks_out.reshape(n_grp, cap_grp, 2), "grp", split_axis=0, concat_axis=0, tiled=True
        ),
        lax.all_to_all(
            gains_out.reshape(n_grp, cap_grp, 2), "grp", split_axis=0, concat_axis=0, tiled=True
        ),
    )
    relay_rows = rows_in.reshape(slot_count, feature_width)
    relay_picks = picks_in.reshape(slot_count, 2)
    relay_gains = gains_in.reshape(slot_count, 2)
    live_count = 4 * token_count
    slot_live = (relay_picks[:, 0] >= 0).astype(jnp.int32)
    slot_order = jnp.cumsum(slot_live) - 1
    packed = (
        (slot_order[None, :] == jnp.arange(live_count)[:, None]) & (slot_live[None, :] > 0)
    ).astype(jnp.int32)
    packed_rows = jnp.dot(
        packed.astype(jnp.bfloat16), relay_rows, preferred_element_type=jnp.float32
    ).astype(jnp.bfloat16)
    packed_picks = jnp.dot(packed, relay_picks)
    packed_gains = jnp.dot(
        packed.astype(jnp.bfloat16), relay_gains, preferred_element_type=jnp.float32
    ).astype(jnp.bfloat16)
    group_rows, group_picks, group_gains = (
        lax.all_gather(packed_rows, "dev", axis=0, tiled=True),
        lax.all_gather(packed_picks, "dev", axis=0, tiled=True),
        lax.all_gather(packed_gains, "dev", axis=0, tiled=True),
    )
    gathered_count = group_rows.shape[0]
    chosen = jnp.sum((group_picks == lax.axis_index("dev")).astype(jnp.int32), axis=1)
    expert_seat = jnp.cumsum(chosen) - 1
    seat_source = seat_sources(expert_seat, chosen > 0, seat_total)
    seat_live = seat_source < gathered_count
    taken_rows = jnp.take(group_rows, jnp.minimum(seat_source, gathered_count - 1), axis=0)
    expert_in = jnp.where(seat_live[:, None], taken_rows, zero_half)
    expert_out = expert_rows(
        expert_in.reshape(n_dev, cap_exp, feature_width), w_first, w_second
    ).reshape(seat_total, feature_width)
    spread_rows = jnp.take(expert_out, jnp.clip(expert_seat, 0, seat_total - 1), axis=0)
    spread = jnp.where((chosen > 0)[:, None], spread_rows, zero_half)
    back = lax.all_to_all(
        spread.reshape(n_dev, live_count, feature_width),
        "dev",
        split_axis=0,
        concat_axis=0,
        tiled=True,
    )
    match = (packed_picks[None, :, :] == jnp.arange(n_dev)[:, None, None]).astype(jnp.float32)
    row_weights = jnp.sum(match * packed_gains.astype(jnp.float32)[None, :, :], axis=2)
    packed_sum = jnp.sum(row_weights[:, :, None] * back.astype(jnp.float32), axis=0)
    partial_value = contract_rows(packed.astype(jnp.float32), packed_sum)
    returned_sums = lax.all_to_all(
        partial_value.reshape(n_grp, cap_grp, feature_width),
        "grp",
        split_axis=0,
        concat_axis=0,
        tiled=True,
    )
    mixed = contract_rows(
        token_hot.astype(jnp.float32), returned_sums.reshape(slot_count, feature_width)
    )
    return mixed.astype(jnp.bfloat16)


def solution(mesh):
    return jax.shard_map(
        per_device,
        mesh=mesh,
        in_specs=(
            P(("grp", "dev"), None),
            P(("grp", "dev"), None),
            P(("grp", "dev"), None),
            P(("grp", "dev"), None, None),
            P(("grp", "dev"), None, None),
        ),
        out_specs=P(("grp", "dev"), None),
        check_vma=False,
    )
```

profile of v0, /device:TPU:6, one launch (start us, length us, event | category | flops | bytes accessed | tf_op | source)
XLA Modules:
  0.0 426.4 jit_solution(9296313556347692572)
XLA Ops:
  6.5 0.8 copy.40
  7.3 0.1 reshape.290
  7.4 0.2 slice_reduce_fusion
  7.6 0.6 reduce-window.24
  8.2 0.2 slice_reduce_fusion.1
  8.5 0.1 fusion.44
  8.6 0.6 convolution_add_fusion
  9.2 0.1 reshape.292
  9.3 0.7 copy.43
  10.0 18.8 %all-to-all-start = ((s32[64,12,2]{1,2,0:T(2,128)}), s32[64,12,2]{1,2,0:T(2,128)S(1)}, u32[]{:S(2)}, u32[]{:S(2)}) async-start(s32[64,12,2]{1,2,0:T(2,128)} %copy.43), calls=%async_computation | async-start | bytes 131072 | tf_op jit(solution)/shard_map/all_to_all | solution.py:75
  28.8 0.1 squeeze.16
  28.9 0.1 reduce_sum.48
  29.1 0.2 convert_reduce_fusion
  29.3 0.5 convolution_convert_fusion.1
  29.8 1.3 reshape.303
  31.1 10.6 %all-to-all-done = s32[64,12,2]{1,2,0:T(2,128)S(1)} async-done(((s32[64,12,2]{1,2,0:T(2,128)}), s32[64,12,2]{1,2,0:T(2,128)S(1)}, u32[]{:S(2)}, u32[]{:S(2)}) %all-to-all-start) | async-done | bytes 6176 | tf_op jit(solution)/shard_map/all_to_all | solution.py:75
  41.7 6.4 %all-to-all-start.2 = ((bf16[64,12,768]{2,1,0:T(8,128)(2,1)}), bf16[64,12,768]{2,1,0:T(8,128)(2,1)S(1)}, u32[]{:S(2)}, u32[]{:S(2)}) async-start(bf16[64,12,768]{2,1,0:T(8,128)(2,1)} %reshape.303), calls=%async_computation.2 | async-start | bytes 3145728 | tf_op jit(solution)/shard_map/all_to_all | solution.py:68
  48.2 0.1 reshape.293
  48.3 0.3 reduce-window.26
  48.7 0.1 slice_reduce_fusion.3
  48.9 74.3 %all-to-all-done.2 = bf16[64,12,768]{2,1,0:T(8,128)(2,1)S(1)} async-done(((bf16[64,12,768]{2,1,0:T(8,128)(2,1)}), bf16[64,12,768]{2,1,0:T(8,128)(2,1)S(1)}, u32[]{:S(2)}, u32[]{:S(2)}) %all-to-all-start.2) | async-done | bytes 1179680 | tf_op jit(solution)/shard_map/all_to_all | solution.py:68
  123.2 0.3 reshape.304
  123.5 1.3 convolution_convert_fusion.2
  124.8 0.1 copy.47
  124.9 0.1 reshape.295
  125.0 0.2 convolution_convert_fusion.4
  125.2 0.1 reshape.296
  125.4 0.6 copy.48
  126.0 6.9 %all-to-all-start.1 = ((bf16[64,12,2]{1,2,0:T(2,128)(2,1)}), bf16[64,12,2]{1,2,0:T(2,128)(2,1)S(1)}, u32[]{:S(2)}, u32[]{:S(2)}) async-start(bf16[64,12,2]{1,2,0:T(2,128)(2,1)} %copy.48), calls=%async_computation.1 | async-start | bytes 65536 | tf_op jit(solution)/shard_map/all_to_all | solution.py:78
  132.9 0.6 fusion.19
  133.5 12.1 %all_gather.6 = s32[2048,2]{0,1:T(2,128)S(1)} all-gather(s32[256,2]{0,1:T(2,128)S(1)} %fusion.19), channel_id=1, replica_groups=mesh['grp'=64,'dev'=8] {'dev'}, dimensions={0}, use_global_device_ids=true | all-gather | bytes 18432 | tf_op jit(solution)/shard_map/all_gather | solution.py:100
  145.6 0.3 reduce-window.36
  146.0 0.1 slice_reduce_fusion.2
  146.2 0.1 reshape.300
  146.2 0.1 copy.50
  146.4 8.0 %scatter_custom_fusion = s32[1536]{0:T(1024)S(1)} fusion(s32[2048]{0:T(1024)S(1)} %bitcast.90, s32[2048]{0:T(1024)S(1)} %iota.29, s32[]{:T(128)} %constant.103.clone.1), kind=kCustom, calls=%fused_computation.109 | custom fusion | bytes 6148 | tf_op jit(solution)/shard_map/scatter | solution.py:36
  154.5 0.1 broadcast_in_dim.74
  154.6 0.1 broadcast_in_dim.76
  154.8 9.0 %gather_fusion = bf16[1536,768]{1,0:T(8,128)(2,1)} fusion(bf16[2048,768]{1,0:T(8,128)(2,1)} %all-gather.2.cloned.1.call-done, s32[2048]{0:T(1024)S(1)} %pad_clamp_fusion), kind=kCustom, calls=%fused_computation | custom fusion | bytes 4724736 | tf_op jit(solution)/shard_map/jit(_take)/gather | solution.py:108
  163.8 3.0 select_select_fusion.1
  166.8 29.7 %while.11 = (s32[]{:T(128)}, bf16[8,192,768]{2,1,0:T(8,128)(2,1)S(1)}, bf16[8,192,768]{2,1,0:T(8,128)(2,1)}, bf16[768,1536]{1,0:T(8,128)(2,1)}, bf16[1536,768]{1,0:T(8,128)(2,1)}) while((s32[]{:T(128)}, bf16[8,192,768]{2,1,0:T(8,128)(2,1)S(1)}, bf16[8,192,768]{2,1,0:T(8,128)(2,1)}, bf16[768,1536]{1,0:T(8,128)(2,1)}, ...), condition=%wide.region_12.13_spmd.clone, body=%wide.region_11.12_spmd.sunk.clone | while | flops 906706944 | bytes 5309509 | solution.py:29
  166.8 3.7 fusion.84
  170.5 3.7 fusion.84
  174.2 3.7 fusion.84
  177.9 3.7 fusion.84
  181.7 3.7 fusion.84
  185.4 3.7 fusion.84
  189.1 3.7 fusion.84
  192.8 3.7 fusion.84
  196.5 9.4 %gather_fusion.1 = bf16[2048,768]{1,0:T(8,128)(2,1)} fusion(bf16[1536,768]{1,0:T(8,128)(2,1)S(1)} %bitcast.82, s32[2048]{0:T(1024)S(1)} %broadcast_clamp_fusion), kind=kCustom, calls=%fused_computation.1 | custom fusion | bytes 6299648 | tf_op jit(solution)/shard_map/jit(_take)/gather | solution.py:113
  205.9 3.5 select_select_fusion
  209.3 3.8 all-to-all-start.3
  213.2 0.1 reshape.297
  213.3 0.1 gt.37
  213.4 0.1 copy.46
  213.6 0.1 sub.39
  213.8 0.2 fusion.11
  214.0 37.3 %all-to-all-done.3 = bf16[8,256,768]{2,1,0:T(8,128)(2,1)S(1)} async-done(((bf16[8,256,768]{2,1,0:T(8,128)(2,1)}), bf16[8,256,768]{2,1,0:T(8,128)(2,1)S(1)}, u32[]{:S(2)}, u32[]{:S(2)}) %all-to-all-start.3) | async-done | bytes 3145760 | tf_op jit(solution)/shard_map/all_to_all | solution.py:115
  251.4 0.6 multiply_reduce_fusion
  252.0 2.2 fusion.12
  254.2 1.4 copy.51
  255.7 158.5 %all_to_all.25 = f32[64,12,768]{2,1,0:T(8,128)S(1)} all-to-all(f32[64,12,768]{2,1,0:T(8,128)S(1)} %copy.51), channel_id=1, replica_groups=mesh['grp'=64,'dev'=8] {'grp'}, dimensions={0} | all-to-all | bytes 4718592 | tf_op jit(solution)/shard_map/all_to_all | solution.py:126
  414.2 1.5 reshape.306
  415.7 3.9 convolution_convert_fusion.3
  (39 shorter events, 1.0 us)
Async XLA Ops:
  6.5 22.8 %copy-start = (bf16[64,768]{1,0:T(8,128)(2,1)S(1)}, bf16[64,768]{1,0:T(8,128)(2,1)}, u32[]{:S(2)}) copy-start(bf16[64,768]{1,0:T(8,128)(2,1)} %param.7) | copy-start | bytes 294916
  10.0 31.7 %all-to-all-start = ((s32[64,12,2]{1,2,0:T(2,128)}), s32[64,12,2]{1,2,0:T(2,128)S(1)}, u32[]{:S(2)}, u32[]{:S(2)}) async-start(s32[64,12,2]{1,2,0:T(2,128)} %copy.43), calls=%async_computation | async-start | bytes 131072 | tf_op jit(solution)/shard_map/all_to_all | solution.py:75
  41.7 81.5 %all-to-all-start.2 = ((bf16[64,12,768]{2,1,0:T(8,128)(2,1)}), bf16[64,12,768]{2,1,0:T(8,128)(2,1)S(1)}, u32[]{:S(2)}, u32[]{:S(2)}) async-start(bf16[64,12,768]{2,1,0:T(8,128)(2,1)} %reshape.303), calls=%async_computation.2 | async-start | bytes 3145728 | tf_op jit(solution)/shard_map/all_to_all | solution.py:68
  48.2 106.7 %all-gather.2.cloned.1.call-start = ((), (), s32[]{:S(2)}) async-start(), calls=%async_computation.5 | async-start | bytes 3538944 | tf_op jit(solution)/shard_map/all_gather | solution.py:99
  48.9 75.8 %copy-start.1 = (bf16[64,8]{0,1:T(8,128)(2,1)S(1)}, bf16[64,8]{0,1:T(8,128)(2,1)}, u32[]{:S(2)}) copy-start(bf16[64,8]{0,1:T(8,128)(2,1)} %param.9) | copy-start | bytes 3076
  126.0 83.3 %all-to-all-start.1 = ((bf16[64,12,2]{1,2,0:T(2,128)(2,1)}), bf16[64,12,2]{1,2,0:T(2,128)(2,1)S(1)}, u32[]{:S(2)}, u32[]{:S(2)}) async-start(bf16[64,12,2]{1,2,0:T(2,128)(2,1)} %copy.48), calls=%async_computation.1 | async-start | bytes 65536 | tf_op jit(solution)/shard_map/all_to_all | solution.py:78
  209.3 42.0 %all-to-all-start.3 = ((bf16[8,256,768]{2,1,0:T(8,128)(2,1)}), bf16[8,256,768]{2,1,0:T(8,128)(2,1)S(1)}, u32[]{:S(2)}, u32[]{:S(2)}) async-start(bf16[8,256,768]{2,1,0:T(8,128)(2,1)} %select_select_fusion), calls=%async_computation.3 | async-start | bytes 6291456 | tf_op jit(solution)/shard_map/all_to_all | solution.py:115
Sparse Core Ops, SparseCore 0:
  124.9 28.0 all-gather.1
where the time goes:
time: 427 us; the launch traced here: 426 us
  blocking collectives  171 us (40%)
  waiting for transfers between devices  122 us (29%)
  matrix products  38.9 us (9%)
  starting transfers between devices  36 us (8%)
  local copies, waits for them, and re-layouts  35.5 us (8%)
  between operations  13.7 us (3%)
  other arithmetic  9.29 us (2%)
    all_to_all x1, blocking collectives, per_device(): lax.all_to_all(partial_value.reshape(n_grp, cap_grp, feature_width), 'grp...  159 us
    all_to_all x1, waiting for transfers between devices, per_device(): lax.all_to_all(rows_out.reshape(n_grp, cap_grp, feature_width), 'grp', sp...  74.3 us
    all_to_all x1, waiting for transfers between devices, per_device(): lax.all_to_all(spread.reshape(n_dev, live_count, feature_width), 'dev', s...  37.3 us
    dot_general x8, matrix products, one_block(): jnp.dot(hidden, w_second, preferred_element_type=jnp.float32)  29.5 us
    all_to_all x1, starting transfers between devices, per_device(): lax.all_to_all(picks_out.reshape(n_grp, cap_grp, 2), 'grp', split_axis=0,...  18.8 us
    all_gather x1, blocking collectives, per_device(): lax.all_gather(packed_picks, 'dev', axis=0, tiled=True)  12.1 us
    all_to_all x1, waiting for transfers between devices, per_device(): lax.all_to_all(picks_out.reshape(n_grp, cap_grp, 2), 'grp', split_axis=0,...  10.6 us
    gather x1, local copies, waits for them, and re-layouts, per_device(): jnp.take(expert_out, jnp.clip(expert_seat, 0, seat_total - 1), axis=0)  9.38 us
  transfers between devices with their start and end apart: 5, of which 3 were waited for; matrix products, arithmetic and copies ran while one was open for 16% of the time, Pallas kernels for 0%

commit v1 on v0

--- a/solution.py
+++ b/solution.py
@@ -2,6 +2,11 @@
 import jax.numpy as jnp
 from jax import lax
 from jax.sharding import PartitionSpec as P
+
+
+def exchange_gather(x, name, dim):
+    stack = jnp.stack([x] * lax.axis_size(name))
+    return jnp.concatenate(lax.all_to_all(stack, name, 0, 0), axis=dim)
 
 
 def earlier_count(onehot):
@@ -97,7 +102,7 @@
     ).astype(jnp.bfloat16)
     group_rows, group_picks, group_gains = (
         lax.all_gather(packed_rows, "dev", axis=0, tiled=True),
-        lax.all_gather(packed_picks, "dev", axis=0, tiled=True),
+        exchange_gather(packed_picks, "dev", 0),
         lax.all_gather(packed_gains, "dev", axis=0, tiled=True),
     )
     gathered_count = group_rows.shape[0]

time: 427 us -> 426 us (level)
  blocking collectives: 171 us -> 159 us
  waiting for transfers between devices: 122 us -> 127 us
  starting transfers between devices: 36 us -> 40.4 us
    all_gather x1 -> x0, blocking collectives: 12.1 us -> none  [per_device(): lax.all_gather(packed_picks, 'dev', axis=0, tiled=True)]
    all_to_all x0 -> x1, starting transfers between devices: none -> 4.47 us  [exchange_gather(): return jnp.concatenate(lax.all_to_all(stack, name, 0, 0), axis=dim)]
    all_to_all x0 -> x1, waiting for transfers between devices: none -> 4.33 us  [exchange_gather(): return jnp.concatenate(lax.all_to_all(stack, name, 0, 0), axis=dim)]
  transfers between devices with their start and end apart: 5 -> 6, of which waited for: 3 -> 5; matrix products, arithmetic and copies ran while one was open for 16% -> 16% of each run, Pallas kernels for 0% -> 0%
where the time goes in v1:
time: 426 us; the launch traced here: 425 us
  blocking collectives  159 us (37%)
  waiting for transfers between devices  127 us (30%)
  starting transfers between devices  40.4 us (9%)
  matrix products  39 us (9%)
  local copies, waits for them, and re-layouts  36.1 us (8%)
  between operations  13.7 us (3%)
  other arithmetic  9.34 us (2%)
    all_to_all x1, blocking collectives, per_device(): lax.all_to_all(partial_value.reshape(n_grp, cap_grp, feature_width), 'grp...  159 us
    all_to_all x1, waiting for transfers between devices, per_device(): lax.all_to_all(rows_out.reshape(n_grp, cap_grp, feature_width), 'grp', sp...  74.3 us
    all_to_all x1, waiting for transfers between devices, per_device(): lax.all_to_all(spread.reshape(n_dev, live_count, feature_width), 'dev', s...  37.3 us
    dot_general x8, matrix products, one_block(): jnp.dot(hidden, w_second, preferred_element_type=jnp.float32)  29.5 us
    all_to_all x1, starting transfers between devices, per_device(): lax.all_to_all(picks_out.reshape(n_grp, cap_grp, 2), 'grp', split_axis=0,...  18.8 us
    all_to_all x1, waiting for transfers between devices, per_device(): lax.all_to_all(picks_out.reshape(n_grp, cap_grp, 2), 'grp', split_axis=0,...  10.6 us
    gather x1, local copies, waits for them, and re-layouts, per_device(): jnp.take(expert_out, jnp.clip(expert_seat, 0, seat_total - 1), axis=0)  9.38 us
    gather x1, local copies, waits for them, and re-layouts, per_device(): jnp.take(group_rows, jnp.minimum(seat_source, gathered_count - 1), axis=0)  8.99 us
  transfers between devices with their start and end apart: 6, of which 5 were waited for; matrix products, arithmetic and copies ran while one was open for 16% of the time, Pallas kernels for 0%

profile of v1, /device:TPU:6, one launch (start us, length us, event | category | flops | bytes accessed | tf_op | source)
XLA Modules:
  0.0 425.3 jit_solution(8544348209032621251)
XLA Ops:
  6.5 0.8 copy.38
  7.4 0.2 slice_reduce_fusion
  7.6 0.6 reduce-window.24
  8.2 0.2 slice_reduce_fusion.1
  8.5 0.1 fusion.44
  8.6 0.6 convolution_add_fusion
  9.2 0.1 reshape.299
  9.3 0.7 copy.41
  10.0 18.8 %all-to-all-start = ((s32[64,12,2]{1,2,0:T(2,128)}), s32[64,12,2]{1,2,0:T(2,128)S(1)}, u32[]{:S(2)}, u32[]{:S(2)}) async-start(s32[64,12,2]{1,2,0:T(2,128)} %copy.41), calls=%async_computation | async-start | bytes 131072 | tf_op jit(solution)/shard_map/all_to_all | solution.py:80
  28.8 0.1 reduce_sum.48
  28.9 0.1 squeeze.16
  29.1 0.2 convert_reduce_fusion
  29.3 0.5 convolution_convert_fusion.1
  29.8 1.3 reshape.310
  31.1 10.6 %all-to-all-done = s32[64,12,2]{1,2,0:T(2,128)S(1)} async-done(((s32[64,12,2]{1,2,0:T(2,128)}), s32[64,12,2]{1,2,0:T(2,128)S(1)}, u32[]{:S(2)}, u32[]{:S(2)}) %all-to-all-start) | async-done | bytes 6176 | tf_op jit(solution)/shard_map/all_to_all | solution.py:80
  41.7 6.4 %all-to-all-start.3 = ((bf16[64,12,768]{2,1,0:T(8,128)(2,1)}), bf16[64,12,768]{2,1,0:T(8,128)(2,1)S(1)}, u32[]{:S(2)}, u32[]{:S(2)}) async-start(bf16[64,12,768]{2,1,0:T(8,128)(2,1)} %reshape.310), calls=%async_computation.3 | async-start | bytes 3145728 | tf_op jit(solution)/shard_map/all_to_all | solution.py:73
  48.2 0.1 reshape.300
  48.3 0.3 reduce-window.26
  48.7 0.1 slice_reduce_fusion.3
  48.9 74.3 %all-to-all-done.3 = bf16[64,12,768]{2,1,0:T(8,128)(2,1)S(1)} async-done(((bf16[64,12,768]{2,1,0:T(8,128)(2,1)}), bf16[64,12,768]{2,1,0:T(8,128)(2,1)S(1)}, u32[]{:S(2)}, u32[]{:S(2)}) %all-to-all-start.3) | async-done | bytes 1179680 | tf_op jit(solution)/shard_map/all_to_all | solution.py:73
  123.2 0.3 reshape.311
  123.5 1.3 convolution_convert_fusion.2
  124.8 0.1 copy.45
  124.9 0.1 reshape.302
  125.0 0.6 fusion.19
  125.5 0.6 eq.108
  126.1 4.5 %all-to-all-start.2 = ((s32[8,256,2]{1,2,0:T(2,128)}), s32[8,256,2]{1,2,0:T(2,128)S(1)}, u32[]{:S(2)}, u32[]{:S(2)}) async-start(s32[8,256,2]{1,2,0:T(2,128)} %eq.108), calls=%async_computation.2 | async-start | bytes 32768 | tf_op jit(solution)/shard_map/all_to_all | solution.py:9
  130.6 0.2 convolution_convert_fusion.4
  130.8 0.1 reshape.303
  131.0 0.6 copy.46
  131.6 4.3 %all-to-all-done.2 = s32[8,256,2]{1,2,0:T(2,128)S(1)} async-done(((s32[8,256,2]{1,2,0:T(2,128)}), s32[8,256,2]{1,2,0:T(2,128)S(1)}, u32[]{:S(2)}, u32[]{:S(2)}) %all-to-all-start.2) | async-done | bytes 16416 | tf_op jit(solution)/shard_map/all_to_all | solution.py:9
  136.0 6.9 %all-to-all-start.1 = ((bf16[64,12,2]{1,2,0:T(2,128)(2,1)}), bf16[64,12,2]{1,2,0:T(2,128)(2,1)S(1)}, u32[]{:S(2)}, u32[]{:S(2)}) async-start(bf16[64,12,2]{1,2,0:T(2,128)(2,1)} %copy.46), calls=%async_computation.1 | async-start | bytes 65536 | tf_op jit(solution)/shard_map/all_to_all | solution.py:83
  142.9 0.3 reduce-window.36
  143.3 0.1 slice_reduce_fusion.2
  143.6 0.1 compare_and_fusion.1
  143.8 8.0 %scatter_custom_fusion = s32[1536]{0:T(1024)S(1)} fusion(s32[2048]{0:T(1024)S(1)} %bitcast.93, s32[2048]{0:T(1024)S(1)} %iota.29, s32[]{:T(128)} %constant.103.clone.1), kind=kCustom, calls=%fused_computation.108 | custom fusion | bytes 6148 | tf_op jit(solution)/shard_map/scatter | solution.py:41
  151.9 0.1 broadcast_in_dim.74
  152.1 0.8 all-gather.2.cloned.1.call-done
  152.9 9.0 %gather_fusion = bf16[1536,768]{1,0:T(8,128)(2,1)} fusion(bf16[2048,768]{1,0:T(8,128)(2,1)} %all-gather.2.cloned.1.call-done, s32[2048]{0:T(1024)S(1)} %pad_clamp_fusion), kind=kCustom, calls=%fused_computation | custom fusion | bytes 4724736 | tf_op jit(solution)/shard_map/jit(_take)/gather | solution.py:113
  161.9 3.0 select_select_fusion.1
  164.9 29.7 %while.11 = (s32[]{:T(128)}, bf16[8,192,768]{2,1,0:T(8,128)(2,1)S(1)}, bf16[8,192,768]{2,1,0:T(8,128)(2,1)}, bf16[768,1536]{1,0:T(8,128)(2,1)}, bf16[1536,768]{1,0:T(8,128)(2,1)}) while((s32[]{:T(128)}, bf16[8,192,768]{2,1,0:T(8,128)(2,1)S(1)}, bf16[8,192,768]{2,1,0:T(8,128)(2,1)}, bf16[768,1536]{1,0:T(8,128)(2,1)}, ...), condition=%wide.region_12.13_spmd.clone, body=%wide.region_11.12_spmd.sunk.clone | while | flops 906706944 | bytes 5309501 | solution.py:34
  164.9 3.7 fusion.85
  168.6 3.7 fusion.85
  172.3 3.7 fusion.85
  176.0 3.7 fusion.85
  179.7 3.7 fusion.85
  183.4 3.7 fusion.85
  187.1 3.7 fusion.85
  190.9 3.7 fusion.85
  194.6 9.4 %gather_fusion.1 = bf16[2048,768]{1,0:T(8,128)(2,1)} fusion(bf16[1536,768]{1,0:T(8,128)(2,1)S(1)} %bitcast.84, s32[2048]{0:T(1024)S(1)} %broadcast_clamp_fusion), kind=kCustom, calls=%fused_computation.1 | custom fusion | bytes 6299648 | tf_op jit(solution)/shard_map/jit(_take)/gather | solution.py:118
  203.9 3.5 select_select_fusion
  207.4 3.8 all-to-all-start.4
  211.3 0.1 reshape.304
  211.4 0.1 gt.34
  211.6 0.1 sub.39
  211.7 0.1 copy.44
  211.8 0.3 fusion.11
  212.1 37.3 %all-to-all-done.4 = bf16[8,256,768]{2,1,0:T(8,128)(2,1)S(1)} async-done(((bf16[8,256,768]{2,1,0:T(8,128)(2,1)}), bf16[8,256,768]{2,1,0:T(8,128)(2,1)S(1)}, u32[]{:S(2)}, u32[]{:S(2)}) %all-to-all-start.4) | async-done | bytes 3145760 | tf_op jit(solution)/shard_map/all_to_all | solution.py:120
  249.4 0.6 multiply_reduce_fusion
  250.1 2.2 fusion.12
  252.3 1.4 copy.49
  253.7 159.3 %all_to_all.30 = f32[64,12,768]{2,1,0:T(8,128)S(1)} all-to-all(f32[64,12,768]{2,1,0:T(8,128)S(1)} %copy.49), channel_id=1, replica_groups=mesh['grp'=64,'dev'=8] {'grp'}, dimensions={0} | all-to-all | bytes 4718592 | tf_op jit(solution)/shard_map/all_to_all | solution.py:131
  413.0 1.5 reshape.313
  414.6 3.8 convolution_convert_fusion.3
  (41 shorter events, 1.3 us)
Async XLA Ops:
  6.5 22.8 %copy-start = (bf16[64,768]{1,0:T(8,128)(2,1)S(1)}, bf16[64,768]{1,0:T(8,128)(2,1)}, u32[]{:S(2)}) copy-start(bf16[64,768]{1,0:T(8,128)(2,1)} %param.7) | copy-start | bytes 294916
  10.0 31.7 %all-to-all-start = ((s32[64,12,2]{1,2,0:T(2,128)}), s32[64,12,2]{1,2,0:T(2,128)S(1)}, u32[]{:S(2)}, u32[]{:S(2)}) async-start(s32[64,12,2]{1,2,0:T(2,128)} %copy.41), calls=%async_computation | async-start | bytes 131072 | tf_op jit(solution)/shard_map/all_to_all | solution.py:80
  41.7 81.5 %all-to-all-start.3 = ((bf16[64,12,768]{2,1,0:T(8,128)(2,1)}), bf16[64,12,768]{2,1,0:T(8,128)(2,1)S(1)}, u32[]{:S(2)}, u32[]{:S(2)}) async-start(bf16[64,12,768]{2,1,0:T(8,128)(2,1)} %reshape.310), calls=%async_computation.3 | async-start | bytes 3145728 | tf_op jit(solution)/shard_map/all_to_all | solution.py:73
  48.2 104.7 %all-gather.2.cloned.1.call-start = ((), (), s32[]{:S(2)}) async-start(), calls=%async_computation.6 | async-start | bytes 3538944 | tf_op jit(solution)/shard_map/all_gather | solution.py:104
  48.9 75.8 %copy-start.1 = (bf16[64,8]{0,1:T(8,128)(2,1)S(1)}, bf16[64,8]{0,1:T(8,128)(2,1)}, u32[]{:S(2)}) copy-start(bf16[64,8]{0,1:T(8,128)(2,1)} %param.9) | copy-start | bytes 3076
  126.1 9.8 %all-to-all-start.2 = ((s32[8,256,2]{1,2,0:T(2,128)}), s32[8,256,2]{1,2,0:T(2,128)S(1)}, u32[]{:S(2)}, u32[]{:S(2)}) async-start(s32[8,256,2]{1,2,0:T(2,128)} %eq.108), calls=%async_computation.2 | async-start | bytes 32768 | tf_op jit(solution)/shard_map/all_to_all | solution.py:9
  136.0 71.4 %all-to-all-start.1 = ((bf16[64,12,2]{1,2,0:T(2,128)(2,1)}), bf16[64,12,2]{1,2,0:T(2,128)(2,1)S(1)}, u32[]{:S(2)}, u32[]{:S(2)}) async-start(bf16[64,12,2]{1,2,0:T(2,128)(2,1)} %copy.46), calls=%async_computation.1 | async-start | bytes 65536 | tf_op jit(solution)/shard_map/all_to_all | solution.py:83
  207.4 42.0 %all-to-all-start.4 = ((bf16[8,256,768]{2,1,0:T(8,128)(2,1)}), bf16[8,256,768]{2,1,0:T(8,128)(2,1)S(1)}, u32[]{:S(2)}, u32[]{:S(2)}) async-start(bf16[8,256,768]{2,1,0:T(8,128)(2,1)} %select_select_fusion), calls=%async_computation.4 | async-start | bytes 6291456 | tf_op jit(solution)/shard_map/all_to_all | solution.py:120
Sparse Core Ops, SparseCore 0:
  124.9 27.9 all-gather.1
